TPU v7x, 128 devices: a whole 4x4x4 slice. The times are simulated.
128 devices in a mesh: frame: 8 (over x_hi, z), patch: 16 (over y, x_lo, core).
Axes of the slice: x: 4 (x_hi: 2, x_lo: 2; x = x_hi * 2 + x_lo), y: 4, z: 4, core: 2. Of those that a mesh axis runs over, the one named last changes fastest.
Arguments:
- latent: bfloat16 [32768, 1536], P(('frame', 'patch')), parts along dimension 0, may hold values from -6 to 6
- conv_weight: float32 [9, 1536], replicated, may hold values from -4 to 4
- time_table: bfloat16 [50, 4608], replicated
- action_table: bfloat16 [18, 4608], replicated
- timestep: int32 [8], P('frame'), parts along dimension 0, may hold values from 0 to 49
- action: int32 [8], P('frame'), parts along dimension 0, may hold values from 0 to 17
- w_qkv: bfloat16 [1536, 4608], replicated, may hold values from -0.21875 to 0.21875
- w_out: bfloat16 [1536, 1536], replicated, may hold values from -0.15625 to 0.15625
- stale_kv: bfloat16 [32768, 3072], P(('frame', 'patch')), parts along dimension 0
Outputs:
- layer_out: bfloat16 [32768, 1536], P(('frame', 'patch')), parts along dimension 0
- fresh_kv: bfloat16 [32768, 3072], P(('frame', 'patch')), parts along dimension 0
There are 8 independent parts, one for each index of `frame`. A program takes and returns all parts, laid end to end along the dimension named above; an argument that names none is the same for every part. Nothing has to cross between parts.
All inputs are finite; a program needn't handle non-finite values.
Results may differ from a plain program's by a relative error of at most 0.012.
Values may be sent and summed in bfloat16 or wider, within the bound.
No kernel may reach another device: no remote copies, remote signals or barrier semaphores. Data moves between devices by JAX's collectives and lax.ppermute only.
A program may use at most 128 MiB of HBM per device.

v0:
```python
import jax
import jax.numpy as jnp
from jax import lax
from jax.sharding import PartitionSpec as P

HEADS = 24
GRID_W = 64


def padded_2(block, sides, width):
    for axis, dim in sides:
        count = lax.axis_size(axis)
        forward = [(i, i + 1) for i in range(count - 1)]
        backward = [(target, source) for source, target in forward]
        low = lax.ppermute(
            lax.slice_in_dim(block, block.shape[dim] - width, None, axis=dim), axis, forward
        )
        high = lax.ppermute(lax.slice_in_dim(block, 0, width, axis=dim), axis, backward)
        block = jnp.concatenate([low, block, high], axis=dim)
    return block


def lookup(table, index):
    hot = (jnp.arange(table.shape[0], dtype=jnp.int32)[None, :] == index[:, None]).astype(
        table.dtype
    )
    return jnp.dot(hot, table, preferred_element_type=jnp.float32)[0]


def attend(carry, piece, start, query, own_start, own_rows):
    width = piece.shape[1] // 2
    heads = query.shape[1]
    size = query.shape[2]
    count_rows = piece.shape[0]
    block = 512

    def step(turn, state):
        top, total, acc = state
        part_kv = lax.dynamic_slice_in_dim(piece, turn * block, block, 0)
        keys = part_kv[:, :width].reshape(block, heads, size)
        values = part_kv[:, width:].reshape(block, heads, size)
        scores = jnp.einsum(
            "qhe,khe->hqk", query, keys, preferred_element_type=jnp.float32
        ) * size ** (-0.5)
        index_rows = start + turn * block + jnp.arange(block, dtype=jnp.int32)
        inside = (index_rows >= own_start) & (index_rows < own_start + own_rows)
        scores = jnp.where(inside[None, None, :], -jnp.inf, scores)
        new_top = jnp.maximum(top, jnp.max(scores, axis=2))
        factor = jnp.exp(top - new_top)
        expo = jnp.exp(scores - new_top[:, :, None])
        total = total * factor + jnp.sum(expo, axis=2)
        acc = acc * factor[:, :, None] + jnp.einsum(
            "hqk,khe->hqe", expo.astype(jnp.bfloat16), values, preferred_element_type=jnp.float32
        )
        return (new_top, total, acc)

    return lax.fori_loop(0, count_rows // block, step, carry)


def per_device(
    latent, conv_weight, time_table, action_table, timestep, action, w_qkv, w_out, stale_kv
):
    rows, width = latent.shape
    grid = latent.reshape(rows // GRID_W, GRID_W, width)
    extended = padded_2(grid, (("patch", 0),), 1)
    padded = jnp.pad(extended, ((0, 0), (1, 1), (0, 0)))
    nrows = grid.shape[0]
    mixed = grid.astype(jnp.float32)
    for a in range(3):
        for b in range(3):
            mixed = (
                mixed
                + padded[a : a + nrows, b : b + GRID_W].astype(jnp.float32) * conv_weight[3 * a + b]
            )
    mixed = mixed.reshape(rows, width)
    modulation = lookup(time_table, timestep) + lookup(action_table, action)
    shift = modulation[:width]
    scale = modulation[width : 2 * width]
    gate = modulation[2 * width :]
    mean = jnp.mean(mixed, axis=1, keepdims=True)
    var = jnp.mean((mixed - mean) ** 2, axis=1, keepdims=True)
    normed = ((mixed - mean) * lax.rsqrt(var + 1e-06) * (1.0 + scale) + shift).astype(jnp.bfloat16)
    projected = jnp.dot(normed, w_qkv, preferred_element_type=jnp.float32)
    fresh_kv = projected[:, width:].astype(jnp.bfloat16)
    heads = HEADS
    size = width // heads
    query = projected[:, :width].astype(jnp.bfloat16).reshape(rows, heads, size)
    own_keys = fresh_kv[:, :width].reshape(rows, heads, size)
    own_values = fresh_kv[:, width:].reshape(rows, heads, size)
    own_scores = jnp.einsum(
        "qhe,khe->hqk", query, own_keys, preferred_element_type=jnp.float32
    ) * size ** (-0.5)
    top = jnp.max(own_scores, axis=2)
    expo = jnp.exp(own_scores - top[:, :, None])
    total = jnp.sum(expo, axis=2)
    acc = jnp.einsum(
        "hqk,khe->hqe", expo.astype(jnp.bfloat16), own_values, preferred_element_type=jnp.float32
    )
    own_start = lax.axis_index("patch") * rows
    whole = lax.all_gather(stale_kv, "patch", axis=0, tiled=True)
    top, total, acc = attend((top, total, acc), whole, 0, query, own_start, rows)
    result = acc / total[:, :, None]
    attended = jnp.transpose(result, (1, 0, 2)).reshape(rows, width).astype(jnp.bfloat16)
    proj = jnp.dot(attended, w_out, preferred_element_type=jnp.float32)
    layer_out = (mixed + gate * proj).astype(jnp.bfloat16)
    return (layer_out, fresh_kv)


def solution(mesh):
    in_specs = (
        P(("frame", "patch"), None),
        P(),
        P(),
        P(),
        P("frame"),
        P("frame"),
        P(),
        P(),
        P(("frame", "patch"), None),
    )
    out_specs = (P(("frame", "patch"), None), P(("frame", "patch"), None))
    return jax.shard_map(
        per_device, mesh=mesh, in_specs=in_specs, out_specs=out_specs, check_vma=False
    )
```

profile of v0, /device:TPU:1, one launch (start us, length us, event | category | flops | bytes accessed | tf_op | source)
XLA Modules:
  0.0 272.6 jit_solution(17641904580914957175)
XLA Ops:
  7.2 2.7 copy.23
  11.1 4.5 %collective-permute-start = (bf16[1,64,1536]{2,1,0:T(8,128)(2,1)S(1)}, bf16[1,64,1536]{2,1,0:T(8,128)(2,1)S(1)}, u32[]{:S(2)}, u32[]{:S(2)}) collective-permute-start(bf16[1,64,1536]{2,1,0:T(8,128)(2,1)S(1)} %get-tuple-element.206), channel_id=1, source_target_pairs={{0,1},{1,2},{2,3},{3,4},{4,5},{5,6},{6,7},{7,8},{8,9},{9,10},{10,1... | collective-permute-start | bytes 589832 | tf_op jit(solution)/shard_map/ppermute | solution.py:15
  15.6 1.9 collective-permute-start.1
  19.4 3.1 %collective-permute-done.1 = bf16[1,64,1536]{2,1,0:T(8,128)(2,1)S(1)} collective-permute-done((bf16[1,64,1536]{2,1,0:T(8,128)(2,1)S(1)}, bf16[1,64,1536]{2,1,0:T(8,128)(2,1)S(1)}, u32[]{:S(2)}, u32[]{:S(2)}) %collective-permute-start.1) | collective-permute-done | bytes 196640 | tf_op jit(solution)/shard_map/ppermute | solution.py:18
  22.9 2.4 fusion.48
  26.2 9.5 %convolution_convert_fusion = bf16[256,4608]{1,0:T(8,128)(2,1)S(1)} fusion(bf16[256,1536]{1,0:T(8,128)(2,1)S(1)} %fusion.33, bf16[1536,4608]{1,0:T(8,128)(2,1)} %param.17), kind=kOutput, calls=%fused_computation.18 | convolution fusion | flops 3625058304 | bytes 17301504 | tf_op jit(solution)/shard_map/dot_general | solution.py:83
  35.7 1.3 slice.150
  37.1 1.3 fusion.51
  38.4 2.3 copy.21
  41.8 1.6 copy.19
  43.5 2.2 multiply_reduce_fusion
  46.8 2.3 fusion.15
  49.2 104.0 %all-gather.2.cloned.1.call-done = bf16[4096,3072]{0,1:T(8,128)(2,1)} async-done(((bf16[256,3072]{0,1:T(8,128)(2,1)}), bf16[4096,3072]{0,1:T(8,128)(2,1)}) %all-gather.2.cloned.1.call-update) | async-done | bytes 25165840 | tf_op jit(solution)/shard_map/all_gather | solution.py:100
  153.2 106.3 %while.18 = (s32[]{:T(128)}, f32[24,256]{1,0:T(8,128)S(1)}, f32[24,256]{1,0:T(8,128)S(1)}, f32[24,256,64]{1,2,0:T(8,128)}, s32[]{:T(128)}, /*index=5*/s32[]{:T(1...) while((s32[]{:T(128)}, f32[24,256]{1,0:T(8,128)S(1)}, ...), condition=%wide.region_7.8_spmd, body=%wide.region_4.7_spmd.sunk | while | flops 840710144 | bytes 51513544 | solution.py:57
  153.2 2.1 fusion.77
  155.3 3.0 %bitcast_reduce_fusion.2 = (f32[24,256]{1,0:T(8,128)S(1)}, f32[24,512,256]{2,1,0:T(8,128)S(1)}) fusion(pred[512]{0:T(512)(128)(4,1)S(1)} %fusion.76, bf16[512,24,64]{0,2,1:T(8,128)(2,1)S(1)} %bitcast.73, bf16[256,24,64]{0,2,1:T(8,128)(2,1)S(1)} %get-tuple-element.307), kind=kOutput, calls=%fused_computation.1.clone.1 | convolution fusion | flops 412084224 | bytes 14967296 | tf_op jit(solution)/shard_map/while/body/eval_jaxpr/qhe,khe->hqk/dot_general | solution.py:42
  158.3 2.6 fusion.78
  160.9 5.5 %multiply_add_fusion.5 = f32[24,256,64]{1,2,0:T(8,128)} fusion(f32[24,256,64]{1,2,0:T(8,128)} %get-tuple-element.290, bf16[512,24,64]{0,2,1:T(8,128)(2,1)S(1)} %bitcast.74, f32[24,512,256]{2,1,0:T(8,128)S(1)} %get-tuple-element.270, f32[24,256]{1,0:T(8,128)S(1)} %max.9, pred[512]{0:T(512)(128)(4,1)S(1)} %fusion.76, f32[24,256]{1,0:T(8,128)S(1)} %get-tuple-element.273), kind=kOutput, calls=%fused_computation.8.clone.1 | convolution fusion | flops 416022528 | bytes 17351168 | tf_op jit(solution)/shard_map/while/body/eval_jaxpr/hqk,khe->hqe/dot_general | solution.py:52
  166.4 2.1 fusion.77
  168.5 3.0 %bitcast_reduce_fusion.2 = (f32[24,256]{1,0:T(8,128)S(1)}, f32[24,512,256]{2,1,0:T(8,128)S(1)}) fusion(pred[512]{0:T(512)(128)(4,1)S(1)} %fusion.76, bf16[512,24,64]{0,2,1:T(8,128)(2,1)S(1)} %bitcast.73, bf16[256,24,64]{0,2,1:T(8,128)(2,1)S(1)} %get-tuple-element.307), kind=kOutput, calls=%fused_computation.1.clone.1 | convolution fusion | flops 412084224 | bytes 14967296 | tf_op jit(solution)/shard_map/while/body/eval_jaxpr/qhe,khe->hqk/dot_general | solution.py:42
  171.6 2.6 fusion.78
  174.2 5.5 %multiply_add_fusion.5 = f32[24,256,64]{1,2,0:T(8,128)} fusion(f32[24,256,64]{1,2,0:T(8,128)} %get-tuple-element.290, bf16[512,24,64]{0,2,1:T(8,128)(2,1)S(1)} %bitcast.74, f32[24,512,256]{2,1,0:T(8,128)S(1)} %get-tuple-element.270, f32[24,256]{1,0:T(8,128)S(1)} %max.9, pred[512]{0:T(512)(128)(4,1)S(1)} %fusion.76, f32[24,256]{1,0:T(8,128)S(1)} %get-tuple-element.273), kind=kOutput, calls=%fused_computation.8.clone.1 | convolution fusion | flops 416022528 | bytes 17351168 | tf_op jit(solution)/shard_map/while/body/eval_jaxpr/hqk,khe->hqe/dot_general | solution.py:52
  179.7 2.1 fusion.77
  181.8 3.0 %bitcast_reduce_fusion.2 = (f32[24,256]{1,0:T(8,128)S(1)}, f32[24,512,256]{2,1,0:T(8,128)S(1)}) fusion(pred[512]{0:T(512)(128)(4,1)S(1)} %fusion.76, bf16[512,24,64]{0,2,1:T(8,128)(2,1)S(1)} %bitcast.73, bf16[256,24,64]{0,2,1:T(8,128)(2,1)S(1)} %get-tuple-element.307), kind=kOutput, calls=%fused_computation.1.clone.1 | convolution fusion | flops 412084224 | bytes 14967296 | tf_op jit(solution)/shard_map/while/body/eval_jaxpr/qhe,khe->hqk/dot_general | solution.py:42
  184.9 2.6 fusion.78
  187.5 5.5 %multiply_add_fusion.5 = f32[24,256,64]{1,2,0:T(8,128)} fusion(f32[24,256,64]{1,2,0:T(8,128)} %get-tuple-element.290, bf16[512,24,64]{0,2,1:T(8,128)(2,1)S(1)} %bitcast.74, f32[24,512,256]{2,1,0:T(8,128)S(1)} %get-tuple-element.270, f32[24,256]{1,0:T(8,128)S(1)} %max.9, pred[512]{0:T(512)(128)(4,1)S(1)} %fusion.76, f32[24,256]{1,0:T(8,128)S(1)} %get-tuple-element.273), kind=kOutput, calls=%fused_computation.8.clone.1 | convolution fusion | flops 416022528 | bytes 17351168 | tf_op jit(solution)/shard_map/while/body/eval_jaxpr/hqk,khe->hqe/dot_general | solution.py:52
  193.0 2.1 fusion.77
  195.1 3.0 %bitcast_reduce_fusion.2 = (f32[24,256]{1,0:T(8,128)S(1)}, f32[24,512,256]{2,1,0:T(8,128)S(1)}) fusion(pred[512]{0:T(512)(128)(4,1)S(1)} %fusion.76, bf16[512,24,64]{0,2,1:T(8,128)(2,1)S(1)} %bitcast.73, bf16[256,24,64]{0,2,1:T(8,128)(2,1)S(1)} %get-tuple-element.307), kind=kOutput, calls=%fused_computation.1.clone.1 | convolution fusion | flops 412084224 | bytes 14967296 | tf_op jit(solution)/shard_map/while/body/eval_jaxpr/qhe,khe->hqk/dot_general | solution.py:42
  198.1 2.6 fusion.78
  200.8 5.5 %multiply_add_fusion.5 = f32[24,256,64]{1,2,0:T(8,128)} fusion(f32[24,256,64]{1,2,0:T(8,128)} %get-tuple-element.290, bf16[512,24,64]{0,2,1:T(8,128)(2,1)S(1)} %bitcast.74, f32[24,512,256]{2,1,0:T(8,128)S(1)} %get-tuple-element.270, f32[24,256]{1,0:T(8,128)S(1)} %max.9, pred[512]{0:T(512)(128)(4,1)S(1)} %fusion.76, f32[24,256]{1,0:T(8,128)S(1)} %get-tuple-element.273), kind=kOutput, calls=%fused_computation.8.clone.1 | convolution fusion | flops 416022528 | bytes 17351168 | tf_op jit(solution)/shard_map/while/body/eval_jaxpr/hqk,khe->hqe/dot_general | solution.py:52
  206.3 2.1 fusion.77
  208.4 3.0 %bitcast_reduce_fusion.2 = (f32[24,256]{1,0:T(8,128)S(1)}, f32[24,512,256]{2,1,0:T(8,128)S(1)}) fusion(pred[512]{0:T(512)(128)(4,1)S(1)} %fusion.76, bf16[512,24,64]{0,2,1:T(8,128)(2,1)S(1)} %bitcast.73, bf16[256,24,64]{0,2,1:T(8,128)(2,1)S(1)} %get-tuple-element.307), kind=kOutput, calls=%fused_computation.1.clone.1 | convolution fusion | flops 412084224 | bytes 14967296 | tf_op jit(solution)/shard_map/while/body/eval_jaxpr/qhe,khe->hqk/dot_general | solution.py:42
  211.4 2.6 fusion.78
  214.1 5.5 %multiply_add_fusion.5 = f32[24,256,64]{1,2,0:T(8,128)} fusion(f32[24,256,64]{1,2,0:T(8,128)} %get-tuple-element.290, bf16[512,24,64]{0,2,1:T(8,128)(2,1)S(1)} %bitcast.74, f32[24,512,256]{2,1,0:T(8,128)S(1)} %get-tuple-element.270, f32[24,256]{1,0:T(8,128)S(1)} %max.9, pred[512]{0:T(512)(128)(4,1)S(1)} %fusion.76, f32[24,256]{1,0:T(8,128)S(1)} %get-tuple-element.273), kind=kOutput, calls=%fused_computation.8.clone.1 | convolution fusion | flops 416022528 | bytes 17351168 | tf_op jit(solution)/shard_map/while/body/eval_jaxpr/hqk,khe->hqe/dot_general | solution.py:52
  219.6 2.1 fusion.77
  221.7 3.0 %bitcast_reduce_fusion.2 = (f32[24,256]{1,0:T(8,128)S(1)}, f32[24,512,256]{2,1,0:T(8,128)S(1)}) fusion(pred[512]{0:T(512)(128)(4,1)S(1)} %fusion.76, bf16[512,24,64]{0,2,1:T(8,128)(2,1)S(1)} %bitcast.73, bf16[256,24,64]{0,2,1:T(8,128)(2,1)S(1)} %get-tuple-element.307), kind=kOutput, calls=%fused_computation.1.clone.1 | convolution fusion | flops 412084224 | bytes 14967296 | tf_op jit(solution)/shard_map/while/body/eval_jaxpr/qhe,khe->hqk/dot_general | solution.py:42
  224.7 2.6 fusion.78
  227.4 5.5 %multiply_add_fusion.5 = f32[24,256,64]{1,2,0:T(8,128)} fusion(f32[24,256,64]{1,2,0:T(8,128)} %get-tuple-element.290, bf16[512,24,64]{0,2,1:T(8,128)(2,1)S(1)} %bitcast.74, f32[24,512,256]{2,1,0:T(8,128)S(1)} %get-tuple-element.270, f32[24,256]{1,0:T(8,128)S(1)} %max.9, pred[512]{0:T(512)(128)(4,1)S(1)} %fusion.76, f32[24,256]{1,0:T(8,128)S(1)} %get-tuple-element.273), kind=kOutput, calls=%fused_computation.8.clone.1 | convolution fusion | flops 416022528 | bytes 17351168 | tf_op jit(solution)/shard_map/while/body/eval_jaxpr/hqk,khe->hqe/dot_general | solution.py:52
  232.9 2.1 fusion.77
  235.0 3.0 %bitcast_reduce_fusion.2 = (f32[24,256]{1,0:T(8,128)S(1)}, f32[24,512,256]{2,1,0:T(8,128)S(1)}) fusion(pred[512]{0:T(512)(128)(4,1)S(1)} %fusion.76, bf16[512,24,64]{0,2,1:T(8,128)(2,1)S(1)} %bitcast.73, bf16[256,24,64]{0,2,1:T(8,128)(2,1)S(1)} %get-tuple-element.307), kind=kOutput, calls=%fused_computation.1.clone.1 | convolution fusion | flops 412084224 | bytes 14967296 | tf_op jit(solution)/shard_map/while/body/eval_jaxpr/qhe,khe->hqk/dot_general | solution.py:42
  238.0 2.6 fusion.78
  240.6 5.5 %multiply_add_fusion.5 = f32[24,256,64]{1,2,0:T(8,128)} fusion(f32[24,256,64]{1,2,0:T(8,128)} %get-tuple-element.290, bf16[512,24,64]{0,2,1:T(8,128)(2,1)S(1)} %bitcast.74, f32[24,512,256]{2,1,0:T(8,128)S(1)} %get-tuple-element.270, f32[24,256]{1,0:T(8,128)S(1)} %max.9, pred[512]{0:T(512)(128)(4,1)S(1)} %fusion.76, f32[24,256]{1,0:T(8,128)S(1)} %get-tuple-element.273), kind=kOutput, calls=%fused_computation.8.clone.1 | convolution fusion | flops 416022528 | bytes 17351168 | tf_op jit(solution)/shard_map/while/body/eval_jaxpr/hqk,khe->hqe/dot_general | solution.py:52
  246.2 2.1 fusion.77
  248.3 3.0 %bitcast_reduce_fusion.2 = (f32[24,256]{1,0:T(8,128)S(1)}, f32[24,512,256]{2,1,0:T(8,128)S(1)}) fusion(pred[512]{0:T(512)(128)(4,1)S(1)} %fusion.76, bf16[512,24,64]{0,2,1:T(8,128)(2,1)S(1)} %bitcast.73, bf16[256,24,64]{0,2,1:T(8,128)(2,1)S(1)} %get-tuple-element.307), kind=kOutput, calls=%fused_computation.1.clone.1 | convolution fusion | flops 412084224 | bytes 14967296 | tf_op jit(solution)/shard_map/while/body/eval_jaxpr/qhe,khe->hqk/dot_general | solution.py:42
  251.3 2.6 fusion.78
  253.9 5.5 %multiply_add_fusion.5 = f32[24,256,64]{1,2,0:T(8,128)} fusion(f32[24,256,64]{1,2,0:T(8,128)} %get-tuple-element.290, bf16[512,24,64]{0,2,1:T(8,128)(2,1)S(1)} %bitcast.74, f32[24,512,256]{2,1,0:T(8,128)S(1)} %get-tuple-element.270, f32[24,256]{1,0:T(8,128)S(1)} %max.9, pred[512]{0:T(512)(128)(4,1)S(1)} %fusion.76, f32[24,256]{1,0:T(8,128)S(1)} %get-tuple-element.273), kind=kOutput, calls=%fused_computation.8.clone.1 | convolution fusion | flops 416022528 | bytes 17351168 | tf_op jit(solution)/shard_map/while/body/eval_jaxpr/hqk,khe->hqe/dot_general | solution.py:52
  259.4 1.6 divide_convert_fusion
  261.1 4.7 %fusion.21 = bf16[256,1536]{1,0:T(8,128)(2,1)} fusion(f32[256,1536]{1,0:T(8,128)S(1)} %bitcast.77, bf16[256,1536]{0,1:T(8,128)(2,1)S(1)} %bitcast.82, bf16[1536,1536]{1,0:T(8,128)(2,1)} %param.18, f32[1536]{0:T(1024)S(1)} %get-tuple-element.208), kind=kOutput, calls=%fused_computation.31 | convolution fusion | flops 1209139200 | bytes 7870464 | tf_op jit(solution)/shard_map/dot_general | solution.py:104
  (62 shorter events, 5.5 us)
Async XLA Ops:
  7.2 11.9 %copy-start = (bf16[50,4608]{1,0:T(8,128)(2,1)S(1)}, bf16[50,4608]{1,0:T(8,128)(2,1)}, u32[]{:S(2)}) copy-start(bf16[50,4608]{1,0:T(8,128)(2,1)} %param.13) | copy-start | bytes 1382404
  7.2 146.0 %all-gather.2.cloned.1.call-start = ((), (), s32[]{:S(2)}) async-start(), calls=%async_computation | async-start | bytes 26738688 | tf_op jit(solution)/shard_map/all_gather | solution.py:100
  9.9 1.1 copy-start.2
  9.9 8.9 %copy-start.4 = (bf16[18,4608]{1,0:T(8,128)(2,1)S(1)}, bf16[18,4608]{1,0:T(8,128)(2,1)}, u32[]{:S(2)}) copy-start(bf16[18,4608]{1,0:T(8,128)(2,1)} %param.14) | copy-start | bytes 497668
  9.9 9.3 %copy-start.5 = (f32[9,1536]{1,0:T(8,128)S(1)}, f32[9,1536]{1,0:T(8,128)}, u32[]{:S(2)}) copy-start(f32[9,1536]{1,0:T(8,128)} %param.12) | copy-start | bytes 165892
  11.1 8.4 %collective-permute-start = (bf16[1,64,1536]{2,1,0:T(8,128)(2,1)S(1)}, bf16[1,64,1536]{2,1,0:T(8,128)(2,1)S(1)}, u32[]{:S(2)}, u32[]{:S(2)}) collective-permute-start(bf16[1,64,1536]{2,1,0:T(8,128)(2,1)S(1)} %get-tuple-element.206), channel_id=1, source_target_pairs={{0,1},{1,2},{2,3},{3,4},{4,5},{5,6},{6,7},{7,8},{8,9},{9,10},{10,1... | collective-permute-start | bytes 589832 | tf_op jit(solution)/shard_map/ppermute | solution.py:15
  15.6 7.0 %collective-permute-start.1 = (bf16[1,64,1536]{2,1,0:T(8,128)(2,1)S(1)}, bf16[1,64,1536]{2,1,0:T(8,128)(2,1)S(1)}, u32[]{:S(2)}, u32[]{:S(2)}) collective-permute-start(bf16[1,64,1536]{2,1,0:T(8,128)(2,1)S(1)} %get-tuple-element.207), channel_id=1, source_target_pairs={{1,0},{2,1},{3,2},{4,3},{5,4},{6,5},{7,6},{8,7},{9,8},{10,9},{11,1... | collective-permute-start | bytes 589832 | tf_op jit(solution)/shard_map/ppermute | solution.py:18
  45.7 1.1 copy-start.3
  261.0 4.7 %copy-start.1 = (bf16[50,4608]{1,0:T(8,128)(2,1)S(1)}, bf16[50,4608]{1,0:T(8,128)(2,1)}, u32[]{:S(2)}) copy-start(bf16[50,4608]{1,0:T(8,128)(2,1)} %param.13) | copy-start | bytes 1382404
Sparse Core Ops, SparseCore 0:
  10.1 143.0 all-gather.1
where the time goes:
time: 273 us
  waiting for transfers between devices  107 us (39%)
  matrix products  87.2 us (32%)
  local copies, waits for them, and re-layouts  28.8 us (11%)
  other arithmetic  27.2 us (10%)
  between operations  15.5 us (6%)
  starting transfers between devices  6.47 us (2%)
    all_gather x1, waiting for transfers between devices, per_device(): whole = lax.all_gather(stale_kv, 'patch', axis=0, tiled=True)  104 us
    dot_general x8, matrix products, step(): jnp.einsum('hqk,khe->hqe', expo.astype(jnp.bfloat16), values, preferred_e...  44.1 us
    dot_general x8, matrix products, step(): jnp.einsum('qhe,khe->hqk', query, keys, preferred_element_type=jnp.float32)  24 us
    reduce_sum x8, other arithmetic, step(): total = total * factor + jnp.sum(expo, axis=2)  20.8 us
    slice x8, local copies, waits for them, and re-layouts, step(): values = part_kv[:, width:].reshape(block, heads, size)  16.8 us
    dot_general x1, matrix products, per_device(): projected = jnp.dot(normed, w_qkv, preferred_element_type=jnp.float32)  9.48 us
  transfers between devices with their start and end apart: 3, of which 2 were waited for; matrix products, arithmetic and copies ran while one was open for 10% of the time, Pallas kernels for 0%

commit v1 on v0

v1 whole, which is shorter than its diff:
```python
import functools
import math

import jax
import jax.numpy as jnp
from jax import lax
from jax.experimental import pallas as pl
from jax.experimental.pallas import tpu as pltpu
from jax.sharding import PartitionSpec as P

HEADS = 24
HD = 64
GRID_W = 64
ROWS = 256
D = 1536
CHIPS = 8
GROUP = 3 * HD
STATS = 16
KV_ROWS = 768
QSCALE = 1.0 / math.sqrt(HD)
F32 = jnp.float32
BF16 = jnp.bfloat16
VMEM = pl.BlockSpec(memory_space=pltpu.VMEM)
ANY = pl.BlockSpec(memory_space=pl.ANY)


def mm(a, b):
    return lax.dot_general(a, b, (((1,), (0,)), ((), ())), preferred_element_type=F32)


KEY_ROWS = 384


def pack_kernel(kv_hbm, out_hbm, kv, out, sems):
    reads = []
    for n, (first, count) in enumerate(((0, D), (D, 1024), (D + 1024, 512))):
        cols = pl.ds(first, count)
        reads.append(pltpu.make_async_copy(kv_hbm.at[:, cols], kv.at[:, cols], sems.at[n]))
    for copy in reads:
        copy.start()

    def write(first, count, n):
        rows = pl.ds(first, count)
        copy = pltpu.make_async_copy(out.at[:, rows], out_hbm.at[:, rows], sems.at[n])
        copy.start()
        return copy

    reads[0].wait()
    for j in range(CHIPS):
        out[j, 0:256, :] = kv[:, 128 * j : 128 * (j + 1)]
        col = 1024 + 64 * j
        out[j, 256:KEY_ROWS, :] = jnp.concatenate(
            [kv[0:128, col : col + 64], kv[128:256, col : col + 64]], axis=1
        )
    keys = write(0, KEY_ROWS, 3)
    for t in range(12):
        if t % 8 == 0:
            reads[1 + t // 8].wait()
        vt = kv[:, D + 128 * t : D + 128 * (t + 1)].T
        if t < 8:
            out[t, 384:512, :] = vt[:, 0:128]
            out[t, 576:704, :] = vt[:, 128:256]
        else:
            for half in range(2):
                j = 2 * (t - 8) + half
                part = vt[64 * half : 64 * half + 64]
                out[j, 512:576, :] = part[:, 0:128]
                out[j, 704:768, :] = part[:, 128:256]
    values = write(KEY_ROWS, KV_ROWS - KEY_ROWS, 4)
    keys.wait()
    values.wait()


def pack(stale_kv):
    return pl.pallas_call(
        pack_kernel,
        out_shape=jax.ShapeDtypeStruct((CHIPS, KV_ROWS, 128), BF16),
        in_specs=[ANY],
        out_specs=ANY,
        scratch_shapes=[
            pltpu.VMEM((ROWS, 2 * D), BF16),
            pltpu.VMEM((CHIPS, KV_ROWS, 128), BF16),
            pltpu.SemaphoreType.DMA((5,)),
        ],
        compiler_params=pltpu.CompilerParams(vmem_limit_bytes=54 * 2**20),
        name="pack_kv",
    )(stale_kv)


W_COLS = 512
W_BLOCKS = 3 * D // W_COLS


def qkv_kernel(
    patch_ref,
    step_ref,
    act_ref,
    lat_ref,
    inner_ref,
    outer_ref,
    cw_ref,
    time_ref,
    action_ref,
    w_hbm,
    q_ref,
    kv_ref,
    mixed_ref,
    gate_ref,
    w_buf,
    ext,
    normed,
    sems,
):
    for c in range(W_BLOCKS):
        pltpu.make_async_copy(
            w_hbm.at[:, pl.ds(c * W_COLS, W_COLS)], w_buf.at[c], sems.at[c]
        ).start()
    patch = patch_ref[0]
    first_core = lax.rem(patch, 2) == 0
    inner, outer = inner_ref[...].astype(F32), outer_ref[...].astype(F32)
    ext[0:64, :] = jnp.where(first_core, outer, inner)
    ext[64:320, :] = lat_ref[...].astype(F32)
    ext[320:384, :] = jnp.where(first_core, inner, outer)

    def lookup(table, index):
        count = table.shape[0]
        hot = (lax.broadcasted_iota(jnp.int32, (16, count), 1) == index).astype(BF16)
        return mm(hot, table[...])[0:1, :]

    modulation = lookup(time_ref, step_ref[0]) + lookup(action_ref, act_ref[0])
    gate_ref[...] = modulation[:, 2 * D :]
    place = lax.rem(lax.broadcasted_iota(jnp.int32, (ROWS, 128), 0), GRID_W)
    not_first = place != 0
    not_last = place != GRID_W - 1
    total = jnp.zeros((ROWS, 128), F32)
    for t in range(D // 128):
        cols = slice(128 * t, 128 * (t + 1))
        a = [ext[64 * k : 64 * k + 256, cols] for k in range(3)]
        w = [cw_ref[k : k + 1, cols] for k in range(9)]
        left = a[0] * w[0] + a[1] * w[3] + a[2] * w[6]
        mid = a[0] * w[1] + a[1] * w[4] + a[2] * w[7]
        right = a[0] * w[2] + a[1] * w[5] + a[2] * w[8]
        left = jnp.where(not_first, pltpu.roll(left, 1, 0), 0.0)
        right = jnp.where(not_last, pltpu.roll(right, ROWS - 1, 0), 0.0)
        m = a[1] + mid + left + right
        mixed_ref[:, cols] = m
        total = total + m
    mean = jnp.sum(total, axis=1, keepdims=True) * (1.0 / D)
    square = jnp.zeros((ROWS, 128), F32)
    for t in range(D // 128):
        m = mixed_ref[:, 128 * t : 128 * (t + 1)] - mean
        square = square + m * m
    inv = lax.rsqrt(jnp.sum(square, axis=1, keepdims=True) * (1.0 / D) + 1e-06)
    for t in range(D // 128):
        cols = slice(128 * t, 128 * (t + 1))
        shift = modulation[:, 128 * t : 128 * (t + 1)]
        scale = modulation[:, D + 128 * t : D + 128 * (t + 1)]
        normed[:, cols] = (
            (mixed_ref[:, cols] - mean) * inv * (1.0 + scale) + shift
        ).astype(BF16)
    for c in range(W_BLOCKS):
        pltpu.make_async_copy(
            w_hbm.at[:, pl.ds(c * W_COLS, W_COLS)], w_buf.at[c], sems.at[c]
        ).wait()
        out = mm(normed[...], w_buf[c])
        if c < D // W_COLS:
            qt = (out * QSCALE).astype(BF16).T
            for t in range(W_COLS // 128):
                tile = c * (W_COLS // 128) + t
                if tile < 8:
                    q_ref[tile, 0:128, :] = qt[128 * t : 128 * t + 128]
                else:
                    for half in range(2):
                        first = 128 * t + 64 * half
                        q_ref[2 * (tile - 8) + half, 128:192, :] = qt[first : first + 64]
        else:
            col = c * W_COLS - D
            kv_ref[:, col : col + W_COLS] = out.astype(BF16)


def qkv(patch, timestep, action, latent, inner, outer, conv_weight, time_table, action_table, w_qkv):
    smem = pl.BlockSpec(memory_space=pltpu.SMEM)
    return pl.pallas_call(
        qkv_kernel,
        out_shape=(
            jax.ShapeDtypeStruct((CHIPS, GROUP, ROWS), BF16),
            jax.ShapeDtypeStruct((ROWS, 2 * D), BF16),
            jax.ShapeDtypeStruct((ROWS, D), F32),
            jax.ShapeDtypeStruct((1, D), F32),
        ),
        in_specs=[smem] * 3 + [VMEM] * 6 + [ANY],
        out_specs=(VMEM,) * 4,
        scratch_shapes=[
            pltpu.VMEM((W_BLOCKS, D, W_COLS), BF16),
            pltpu.VMEM((ROWS + 2 * GRID_W, D), F32),
            pltpu.VMEM((ROWS, D), BF16),
            pltpu.SemaphoreType.DMA((W_BLOCKS,)),
        ],
        compiler_params=pltpu.CompilerParams(vmem_limit_bytes=40 * 2**20),
        cost_estimate=pl.CostEstimate(
            flops=40 * 2 * ROWS * D * 3 * D, bytes_accessed=20 * 2**20, transcendentals=0
        ),
        name="conv_norm_qkv",
    )(patch, timestep, action, latent, inner, outer, conv_weight, time_table, action_table, w_qkv)


def own_kernel(q_ref, kv_ref, tie_ref, o_ref, lse_ref, s_a, s_b):
    del tie_ref
    zeros = jnp.zeros((HD, ROWS), BF16)
    ones = jnp.ones((STATS, ROWS), BF16)
    buffers = (s_a, s_b)

    def scores(tile):
        buf = buffers[tile % 2]
        keys = kv_ref[:, 128 * tile : 128 * tile + 128]
        tops = []
        for half in range(2):
            if tile < 8:
                q = q_ref[tile, 64 * half : 64 * half + 64, :]
            else:
                q = q_ref[2 * (tile - 8) + half, 128:192, :]
            q = jnp.concatenate([q, zeros] if half == 0 else [zeros, q], axis=0)
            s = mm(keys, q)
            buf[half] = s
            tops.append(jnp.max(s, axis=0, keepdims=True))
        return tops

    tops = scores(0)
    for tile in range(12):
        now = tops
        if tile < 11:
            tops = scores(tile + 1)
        vt = kv_ref[:, D + 128 * tile : D + 128 * tile + 128].T
        for half in range(2):
            head = 2 * tile + half
            p = jnp.exp(buffers[tile % 2][half] - now[half]).astype(BF16)
            acc = mm(jnp.concatenate([vt[64 * half : 64 * half + 64], ones], axis=0), p)
            total = acc[HD : HD + 1, :]
            o_ref[64 * head : 64 * head + 64, :] = (acc[0:HD, :] * (1.0 / total)).astype(BF16)
            lse_ref[head : head + 1, :] = now[half] + jnp.log(total)


def own(q, kv, tie):
    return pl.pallas_call(
        own_kernel,
        out_shape=(
            jax.ShapeDtypeStruct((D, ROWS), BF16),
            jax.ShapeDtypeStruct((HEADS, ROWS), F32),
        ),
        in_specs=[VMEM] * 2 + [ANY],
        out_specs=(VMEM,) * 2,
        scratch_shapes=[pltpu.VMEM((2, ROWS, ROWS), F32)] * 2,
        compiler_params=pltpu.CompilerParams(vmem_limit_bytes=12 * 2**20),
        cost_estimate=pl.CostEstimate(
            flops=16 * ROWS * ROWS * D, bytes_accessed=4 * 2**20, transcendentals=HEADS * ROWS * ROWS
        ),
        name="own_block",
    )(q, kv, tie)


CHUNK = 3
CHUNKS = 5
PAIR = 2
AHEAD = 2


def split3(x):
    hi = x.astype(BF16)
    rest = x - hi.astype(F32)
    mid = rest.astype(BF16)
    return hi, mid, (rest - mid.astype(F32)).astype(BF16)


def others_kernel(shift, chip_ref, q_ref, same_ref, pair_ref, tie_ref, o_ref, s_a, s_b):
    del tie_ref
    block = lax.rem(chip_ref[0] + shift + pl.program_id(0), CHIPS)
    zeros = jnp.zeros((HD, ROWS), BF16)
    qs = []
    for h in range(3):
        q = q_ref[0, 64 * h : 64 * h + 64, :]
        qs.append(
            (jnp.concatenate([q, zeros], axis=0), jnp.concatenate([zeros, q], axis=0))
        )
    places = [(same_ref, lax.rem(block + 1 + n, CHIPS)) for n in range(CHIPS - 1)]
    places += [(pair_ref, n) for n in range(CHIPS)]

    def key_parts(h, n):
        ref, b = places[n]
        if h < 2:
            return [(ref[b, 0:256, :], h)]
        packed = ref[b, 256:384, :]
        return [(packed, 0), (packed, 1)]

    def value_parts(h, ns):
        parts = []
        for n in ns:
            ref, b = places[n]
            for g in range(2):
                first = 384 + 192 * g + 64 * h
                parts.append(ref[b, first : first + 64, :])
        values = jnp.concatenate(parts, axis=1)
        return jnp.concatenate([values, jnp.ones((STATS, values.shape[1]), BF16)], axis=0)

    def emit(h, acc, top):
        total = acc[HD : HD + 1, :]
        o_ref[0, 64 * h : 64 * h + 64, :] = (acc[0:HD, :] * (1.0 / total)).astype(BF16)
        stats = split3(top + jnp.log(total))
        return list(stats)

    def write_stats(stats):
        stats = stats + [jnp.zeros((STATS - len(stats), ROWS), BF16)]
        o_ref[0, GROUP : GROUP + STATS, :] = jnp.concatenate(stats, axis=0)

    row = lax.broadcasted_iota(jnp.int32, (128, ROWS), 0)
    lanes = jnp.ones((ROWS, 128), BF16)
    first, tops, rhs = [], [], []
    for h in range(3):
        s = jnp.concatenate([mm(k, qs[h][i]) for k, i in key_parts(h, 0)], axis=0)
        top = jnp.max(s, axis=0, keepdims=True).astype(BF16).astype(F32)
        first.append(s)
        tops.append(top)
        minus = jnp.where(row == 0, -top, 0.0).astype(BF16)
        rhs.append([jnp.concatenate([q, minus], axis=0) for q in qs[h]])
    groups = [[0]] + [list(range(n, n + PAIR)) for n in range(1, 15, PAIR)]
    units = [(h, ns) for h in range(3) for ns in groups]

    def relative(h, ns):
        if ns == [0]:
            return first[h] - tops[h]
        outs = []
        for n in ns:
            for k, i in key_parts(h, n):
                outs.append(mm(jnp.concatenate([k, lanes[: k.shape[0]]], axis=1), rhs[h][i]))
        return jnp.concatenate(outs, axis=0)

    acc = [None] * 3
    waiting = [relative(*units[u]) for u in range(AHEAD)]
    for u, (h, ns) in enumerate(units):
        s = waiting.pop(0)
        if u + AHEAD < len(units):
            waiting.append(relative(*units[u + AHEAD]))
        out = mm(value_parts(h, ns), jnp.exp(s).astype(BF16))
        acc[h] = out if acc[h] is None else acc[h] + out
    stats = []
    good = None
    for h in range(3):
        stats += emit(h, acc[h], tops[h])
        total = acc[h][HD : HD + 1, :]
        size = jnp.sum(jnp.abs(acc[h]), axis=0, keepdims=True)
        ok = (total > 2.0**-20) & (total < 2.0**100) & (size < 2.0**126)
        good = ok if good is None else good & ok
    write_stats(stats)

    @pl.when(jnp.max(jnp.where(good, 0.0, 1.0)) > 0.5)
    def _():
        buffers = (s_a, s_b)
        units = [(h, c) for h in range(3) for c in range(CHUNKS)]

        def scores(u):
            h, c = units[u]
            buf = buffers[u % 2]
            top = None
            at = 0
            for n in range(c * CHUNK, (c + 1) * CHUNK):
                for k, i in key_parts(h, n):
                    s = mm(k, qs[h][i])
                    buf[at : at + s.shape[0], :] = s
                    at += s.shape[0]
                    m = jnp.max(s.reshape(-1, 8, ROWS), axis=0)
                    top = m if top is None else jnp.maximum(top, m)
            return jnp.max(top, axis=0, keepdims=True)

        tops = scores(0)
        top = acc = None
        stats = []
        for u, (h, c) in enumerate(units):
            new = tops if c == 0 else jnp.maximum(top, tops)
            if u + 1 < len(units):
                tops = scores(u + 1)
            p = jnp.exp(buffers[u % 2][...] - new).astype(BF16)
            out = mm(value_parts(h, range(c * CHUNK, (c + 1) * CHUNK)), p)
            acc = out if c == 0 else acc * jnp.exp(top - new) + out
            top = new
            if c == CHUNKS - 1:
                stats += emit(h, acc, top)
        write_stats(stats)


def others(chip, q, same, pair, tie, count, shift):
    place = lambda i, c: (lax.rem(c[0] + shift + i, CHIPS), 0, 0)
    out_place = place if count > 1 else lambda i, c: (0, 0, 0)
    return pl.pallas_call(
        functools.partial(others_kernel, shift),
        grid_spec=pltpu.PrefetchScalarGridSpec(
            num_scalar_prefetch=1,
            grid=(count,),
            in_specs=[pl.BlockSpec((1, GROUP, ROWS), place), VMEM, VMEM, ANY],
            out_specs=pl.BlockSpec((1, GROUP + STATS, ROWS), out_place),
            scratch_shapes=[pltpu.VMEM((CHUNK * ROWS, ROWS), F32)] * 2,
        ),
        out_shape=jax.ShapeDtypeStruct((CHIPS if count > 1 else 1, GROUP + STATS, ROWS), BF16),
        compiler_params=pltpu.CompilerParams(vmem_limit_bytes=16 * 2**20),
        cost_estimate=pl.CostEstimate(
            flops=count * 15 * 12 * ROWS * ROWS * HD * 4,
            bytes_accessed=4 * 2**20,
            transcendentals=count * 15 * 3 * ROWS * ROWS,
        ),
        name="other_blocks",
    )(chip, q, same, pair, tie)


def merge_kernel(
    chip_ref, o_ref, local_ref, own_ref, lse_ref, att
):
    part = [
        jnp.where(chip_ref[0] == j, local_ref[0], o_ref[j]).astype(F32) for j in range(CHIPS)
    ]
    for head in range(HEADS):
        if head < 16:
            chip, slot = head // 2, head % 2
        else:
            chip, slot = head - 16, 2
        parts = part[chip][GROUP : GROUP + STATS]
        there = parts[3 * slot : 3 * slot + 1] + parts[3 * slot + 1 : 3 * slot + 2]
        there = there + parts[3 * slot + 2 : 3 * slot + 3]
        here = lse_ref[head : head + 1, :]
        top = jnp.maximum(there, here)
        a = jnp.exp(there - top)
        b = jnp.exp(here - top)
        both = 1.0 / (a + b)
        rows = slice(64 * head, 64 * head + 64)
        merged = (
            part[chip][64 * slot : 64 * slot + 64] * (a * both)
            + own_ref[rows, :].astype(F32) * (b * both)
        )
        att[:, rows] = merged.astype(BF16).T


def merge(chip, o, local, own_o, lse):
    return pl.pallas_call(
        merge_kernel,
        out_shape=jax.ShapeDtypeStruct((ROWS, D), BF16),
        in_specs=[pl.BlockSpec(memory_space=pltpu.SMEM)] + [VMEM] * 4,
        out_specs=VMEM,
        compiler_params=pltpu.CompilerParams(vmem_limit_bytes=10 * 2**20),
        cost_estimate=pl.CostEstimate(
            flops=2**31, bytes_accessed=4 * 2**20, transcendentals=0
        ),
        name="merge",
    )(chip, o, local, own_o, lse)


def output_kernel(att_ref, gate_ref, mixed_ref, w_ref, out_ref):
    halves = 2
    width = D // halves
    for k in range(halves):
        cols = slice(k * width, (k + 1) * width)
        proj = mm(att_ref[...], w_ref[:, cols])
        out_ref[:, cols] = (mixed_ref[:, cols] + gate_ref[:, cols] * proj).astype(BF16)


def output(att, mixed, gate, w_out):
    return pl.pallas_call(
        output_kernel,
        out_shape=jax.ShapeDtypeStruct((ROWS, D), BF16),
        in_specs=[VMEM] * 4,
        out_specs=VMEM,
        compiler_params=pltpu.CompilerParams(vmem_limit_bytes=12 * 2**20),
        cost_estimate=pl.CostEstimate(
            flops=2 * ROWS * D * D, bytes_accessed=10 * 2**20, transcendentals=0
        ),
        name="output_projection",
    )(att, gate, mixed, w_out)


def per_device(
    latent, conv_weight, time_table, action_table, timestep, action, w_qkv, w_out, stale_kv
):
    count = lax.axis_size("patch")
    same_core = [list(range(c, count, 2)) for c in range(2)]

    def exchange(x):
        return lax.all_to_all(x, "patch", 0, 0, tiled=True, axis_index_groups=same_core)

    chip = (lax.axis_index("patch") // 2).astype(jnp.int32).reshape(1)
    patch = lax.axis_index("patch").astype(jnp.int32).reshape(1)
    top_row, last_row = latent[:GRID_W], latent[-GRID_W:]
    even = patch[0] % 2 == 0
    between = [(i, i + 1) for i in range(1, count - 1, 2)]
    packed, outer, inner = lax.optimization_barrier(
        (
            pack(stale_kv),
            jnp.where(even, top_row, last_row),
            jnp.where(even, last_row, top_row),
        )
    )
    outer = lax.ppermute(outer, "patch", between + [(b, a) for a, b in between])
    swap = [(i, i ^ 1) for i in range(count)]
    inner = lax.ppermute(inner, "patch", swap)
    same = exchange(packed)
    q, fresh_kv, mixed, gate = qkv(
        patch, timestep, action, latent, inner, outer, conv_weight, time_table, action_table, w_qkv
    )
    queries = exchange(q)
    same, _ = lax.optimization_barrier((same, gate))
    own_o, lse = own(q, fresh_kv, same)
    pair = lax.ppermute(same, "patch", swap)
    local = others(chip, q, same, pair, lse, 1, 0)
    remote = others(chip, queries, same, pair, local, CHIPS - 1, 1)
    attended = merge(chip, exchange(remote), local, own_o, lse)
    layer_out = output(attended, mixed, gate, w_out)
    return (layer_out, fresh_kv)


def solution(mesh):
    rows = P(("frame", "patch"), None)
    in_specs = (rows, P(), P(), P(), P("frame"), P("frame"), P(), P(), rows)
    return jax.shard_map(
        per_device, mesh=mesh, in_specs=in_specs, out_specs=(rows, rows), check_vma=False
    )
```

time: 273 us -> 126 us (0.46)
  waiting for transfers between devices: 107 us -> 9.79 us
  matrix products: 87.2 us -> 0 us
  Pallas kernels: 0 us -> 79.3 us
  other arithmetic: 27.2 us -> 0.03 us
  local copies, waits for them, and re-layouts: 28.8 us -> 2.32 us
  blocking collectives: 0 us -> 18.3 us
  between operations: 15.5 us -> 2.16 us
  starting transfers between devices: 6.47 us -> 13.9 us
    all_gather x1 -> x0, waiting for transfers between devices: 104 us -> none  [per_device(): whole = lax.all_gather(stale_kv, 'patch', axis=0, tiled=True)]
    dot_general x22 -> x0, matrix products: 87.2 us -> none  [the longest x8 44.1 us: step(): jnp.einsum('hqk,khe->hqe', expo.astype(jnp.bfloat16), values, preferred_e...]
    pallas_call x0 -> x7, Pallas kernels: none -> 79.3 us  [the longest x2 60.3 us: others(): pl.pallas_call(functools.partial(others_kernel, shift), grid_spec=pltpu.P...]
    slice x15 -> x0, local copies, waits for them, and re-layouts: 24.7 us -> none  [the longest x8 16.8 us: step(): values = part_kv[:, width:].reshape(block, heads, size)]
    reduce_sum x11 -> x0, other arithmetic: 24.6 us -> none  [the longest x8 20.8 us: step(): total = total * factor + jnp.sum(expo, axis=2)]
    all_to_all x0 -> x1, blocking collectives: none -> 18.3 us  [exchange(): lax.all_to_all(x, 'patch', 0, 0, tiled=True, axis_index_groups=same_core)]
    all_to_all x0 -> x2, waiting for transfers between devices: none -> 9.78 us  [exchange(): lax.all_to_all(x, 'patch', 0, 0, tiled=True, axis_index_groups=same_core)]
    all_to_all x0 -> x2, starting transfers between devices: none -> 8.44 us  [exchange(): lax.all_to_all(x, 'patch', 0, 0, tiled=True, axis_index_groups=same_core)]
  transfers between devices with their start and end apart: 3 -> 5, of which waited for: 2 -> 1; matrix products, arithmetic and copies ran while one was open for 10% -> 0% of each run, Pallas kernels for 0% -> 18%
where the time goes in v1:
time: 126 us
  Pallas kernels  79.3 us (63%)
  blocking collectives  18.3 us (15%)
  starting transfers between devices  13.9 us (11%)
  waiting for transfers between devices  9.79 us (8%)
  local copies, waits for them, and re-layouts  2.32 us (2%)
  between operations  2.16 us (2%)
    pallas_call x2, Pallas kernels, others(): pl.pallas_call(functools.partial(others_kernel, shift), grid_spec=pltpu.P...  60.3 us
    all_to_all x1, blocking collectives, exchange(): lax.all_to_all(x, 'patch', 0, 0, tiled=True, axis_index_groups=same_core)  18.3 us
    all_to_all x2, waiting for transfers between devices, exchange(): lax.all_to_all(x, 'patch', 0, 0, tiled=True, axis_index_groups=same_core)  9.78 us
    pallas_call x1, Pallas kernels, qkv(): pl.pallas_call(qkv_kernel, out_shape=(jax.ShapeDtypeStruct((CHIPS, GROUP,...  9.68 us
    all_to_all x2, starting transfers between devices, exchange(): lax.all_to_all(x, 'patch', 0, 0, tiled=True, axis_index_groups=same_core)  8.44 us
    pallas_call x1, Pallas kernels, own(): pl.pallas_call(own_kernel, out_shape=(jax.ShapeDtypeStruct((D, ROWS), BF1...  3.4 us
    ppermute x1, starting transfers between devices, per_device(): outer = lax.ppermute(outer, 'patch', between + [(b, a) for a, b in between])  3.23 us
    pallas_call x1, Pallas kernels, pack(): pl.pallas_call(pack_kernel, out_shape=jax.ShapeDtypeStruct((CHIPS, KV_ROW...  2.67 us
  transfers between devices with their start and end apart: 5, of which 1 were waited for; matrix products, arithmetic and copies ran while one was open for 0% of the time, Pallas kernels for 18%

profile of v1, /device:TPU:1, one launch (start us, length us, event | category | flops | bytes accessed | tf_op | source)
XLA Modules:
  0.0 125.8 jit_solution(1302603645216977584)
XLA Ops:
  0.6 0.0 copy-start
  0.7 2.7 %pack_kv.1 = bf16[8,768,128]{2,1,0:T(8,128)(2,1)} custom-call(bf16[256,3072]{1,0:T(8,128)(2,1)} %kv_hbm.1), custom_call_target="tpu_custom_call" | custom-call | tf_op jit(solution)/shard_map/pack_kv/pallas_call | solution.py:75
  3.3 0.0 copy-done
  3.4 0.0 copy-start.1
  3.4 0.0 copy-start.2
  3.4 1.5 %collective-permute-start = (bf16[64,1536]{1,0:T(8,128)(2,1)S(1)}, bf16[64,1536]{1,0:T(8,128)(2,1)S(1)}, u32[]{:S(2)}, u32[]{:S(2)}) collective-permute-start(bf16[64,1536]{1,0:T(8,128)(2,1)S(1)} %get-tuple-element.12), channel_id=1, source_target_pairs={{0,1},{1,0},{2,3},{3,2},{4,5},{5,4},{6,7},{7,6},{8,9},{9,8},{10,11... | collective-permute-start | bytes 589832 | tf_op jit(solution)/shard_map/ppermute | solution.py:499
  4.9 3.2 %collective-permute-start.1 = (bf16[64,1536]{1,0:T(8,128)(2,1)S(1)}, bf16[64,1536]{1,0:T(8,128)(2,1)S(1)}, u32[]{:S(2)}, u32[]{:S(2)}) collective-permute-start(bf16[64,1536]{1,0:T(8,128)(2,1)S(1)} %get-tuple-element.13), channel_id=1, source_target_pairs={{1,2},{3,4},{5,6},{7,8},{9,10},{11,12},{13,14},{2,1},{4,3},{6,5},{... | collective-permute-start | bytes 589832 | tf_op jit(solution)/shard_map/ppermute | solution.py:497
  8.1 4.9 %all-to-all-start.1 = ((bf16[8,768,128]{2,1,0:T(8,128)(2,1)}), bf16[8,768,128]{2,1,0:T(8,128)(2,1)}, u32[]{:S(2)}, u32[]{:S(2)}) async-start(bf16[8,768,128]{2,1,0:T(8,128)(2,1)} %pack_kv.1), calls=%async_computation.1 | async-start | bytes 3145728 | tf_op jit(solution)/shard_map/all_to_all | solution.py:483
  14.3 0.0 collective-permute-done.inner_ref
  14.3 0.0 collective-permute-done.1.outer_ref
  14.4 0.0 copy-done.1
  14.4 0.0 copy-done.2
  14.4 0.0 copy-start.3
  14.4 0.9 copy-done.3
  15.3 9.7 %conv_norm_qkv.1 = (bf16[8,192,256]{2,1,0:T(8,128)(2,1)}, bf16[256,3072]{1,0:T(8,128)(2,1)}, f32[256,1536]{1,0:T(8,128)S(1)}, f32[1,1536]{1,0:T(1,128)S(1)}) custom-call(s32[1]{0:T(128)} %bitcast.1.patch_ref, s32[1]{0:T(128)S(6)} %copy.11.step_ref, s32[1]{0:T(128)S(6)} %copy.12.act_ref, bf16[256,1536]{1,0:T(8,128)(2,1)S(1)} %copy-done, ...), custom_call_target="tpu_custom_call" | custom-call | flops 144955146240 | bytes 20971520 | tf_op jit(solution)/shard_map/conv_norm_qkv/pallas_call | solution.py:183
  25.0 9.8 %all-to-all-done.1.tie_ref.same_ref = bf16[8,768,128]{2,1,0:T(8,128)(2,1)} async-done(((bf16[8,768,128]{2,1,0:T(8,128)(2,1)}), bf16[8,768,128]{2,1,0:T(8,128)(2,1)}, u32[]{:S(2)}, u32[]{:S(2)}) %all-to-all-start.1) | async-done | bytes 1572896 | tf_op jit(solution)/shard_map/all_to_all | solution.py:483
  34.7 0.7 collective-permute-start.2
  35.5 3.5 %all-to-all-start = ((bf16[8,192,256]{2,1,0:T(8,128)(2,1)}), bf16[8,192,256]{2,1,0:T(8,128)(2,1)S(1)}, u32[]{:S(2)}, u32[]{:S(2)}) async-start(bf16[8,192,256]{2,1,0:T(8,128)(2,1)} %get-tuple-element.14.q_ref), calls=%async_computation | async-start | bytes 1572864 | tf_op jit(solution)/shard_map/all_to_all | solution.py:483
  39.0 0.0 copy-start.4
  39.0 1.4 %copy-done.4 = bf16[256,3072]{1,0:T(8,128)(2,1)S(1)} copy-done((bf16[256,3072]{1,0:T(8,128)(2,1)S(1)}, bf16[256,3072]{1,0:T(8,128)(2,1)}, u32[]{:S(2)}) %copy-start.4) | copy-done | bytes 1572888
  40.4 3.4 %own_block.1 = (bf16[1536,256]{1,0:T(8,128)(2,1)S(1)}, f32[24,256]{1,0:T(8,128)S(1)}) custom-call(bf16[8,192,256]{2,1,0:T(8,128)(2,1)} %get-tuple-element.14.q_ref, bf16[256,3072]{1,0:T(8,128)(2,1)S(1)} %copy-done.4, bf16[8,768,128]{2,1,0:T(8,128)(2,1)} %all-to-all-done.1.tie_ref.same_ref), custom_call_target="tpu_custom_call" | custom-call | flops 1610612736 | bytes 4194304 | tf_op jit(solution)/shard_map/own_block/pallas_call | solution.py:244
  43.9 0.0 collective-permute-done.2.pair_ref
  43.9 9.1 %other_blocks.2.tie_ref.local_ref = bf16[1,208,256]{2,1,0:T(8,128)(2,1)S(1)} custom-call(s32[1]{0:T(128)} %bitcast.chip_ref, bf16[8,192,256]{2,1,0:T(8,128)(2,1)} %get-tuple-element.14.q_ref, bf16[8,768,128]{2,1,0:T(8,128)(2,1)} %all-to-all-done.1.tie_ref.same_ref, bf16[8,768,128]{2,1,0:T(8,128)(2,1)} %collective-permute-done.2.pair_ref, ...), custom_call_target="tpu_custom_call" | custom-call | flops 3019898880 | bytes 4194304 | tf_op jit(solution)/shard_map/other_blocks/pallas_call | solution.py:392
  52.9 0.0 all-to-all-done.q_ref
  52.9 51.2 %other_blocks.3 = bf16[8,208,256]{2,1,0:T(8,128)(2,1)S(1)} custom-call(s32[1]{0:T(128)} %bitcast.chip_ref, bf16[8,192,256]{2,1,0:T(8,128)(2,1)S(1)} %all-to-all-done.q_ref, bf16[8,768,128]{2,1,0:T(8,128)(2,1)} %all-to-all-done.1.tie_ref.same_ref, bf16[8,768,128]{2,1,0:T(8,128)(2,1)} %collective-permute-done.2.pair_ref, ...), custom_call_target="tpu_custom_call" | custom-call | flops 21139292160 | bytes 4194304 | tf_op jit(solution)/shard_map/other_blocks/pallas_call | solution.py:392
  104.1 0.0 slice-start
  104.2 18.3 %all_to_all.15.o_ref = bf16[8,208,256]{2,1,0:T(8,128)(2,1)S(1)} all-to-all(bf16[8,208,256]{2,1,0:T(8,128)(2,1)S(1)} %other_blocks.3), channel_id=1, replica_groups={{0,2,4,6,8,10,12,14},{1,3,5,7,9,11,13,15},{16,18,20,22,24,26,28,30},{17..., dimensions={0} | all-to-all | bytes 1703936 | tf_op jit(solution)/shard_map/all_to_all | solution.py:483
  122.5 0.0 slice-start.1
  122.5 1.1 merge.1.att_ref
  123.5 0.0 slice-done
  123.6 0.0 slice-done.1
  123.6 2.3 %output_projection.1 = bf16[256,1536]{1,0:T(8,128)(2,1)} custom-call(bf16[256,1536]{1,0:T(8,128)(2,1)S(1)} %merge.1.att_ref, f32[1,1536]{1,0:T(1,128)S(1)} %get-tuple-element.16.gate_ref, f32[256,1536]{1,0:T(8,128)S(1)} %get-tuple-element.21.mixed_ref, bf16[1536,1536]{1,0:T(8,128)(2,1)S(1)} %bitcast.3), custom_call_target="tpu_custom_call" | custom-call | flops 1207959552 | bytes 10485760 | tf_op jit(solution)/shard_map/output_projection/pallas_call | solution.py:463
  (2 shorter events, 0.0 us)
Async XLA Ops:
  0.6 2.7 %copy-start = (bf16[256,1536]{1,0:T(8,128)(2,1)S(1)}, bf16[256,1536]{1,0:T(8,128)(2,1)}, u32[]{:S(2)}) copy-start(bf16[256,1536]{1,0:T(8,128)(2,1)} %lat_ref.1) | copy-start | bytes 2359300
  3.4 11.0 %copy-start.1 = (bf16[50,4608]{1,0:T(8,128)(2,1)S(1)}, bf16[50,4608]{1,0:T(8,128)(2,1)}, u32[]{:S(2)}) copy-start(bf16[50,4608]{1,0:T(8,128)(2,1)} %time_ref.1) | copy-start | bytes 1382404
  3.4 11.0 %copy-start.2 = (bf16[18,4608]{1,0:T(8,128)(2,1)S(1)}, bf16[18,4608]{1,0:T(8,128)(2,1)}, u32[]{:S(2)}) copy-start(bf16[18,4608]{1,0:T(8,128)(2,1)} %action_ref.1) | copy-start | bytes 497668
  3.4 10.9 %collective-permute-start = (bf16[64,1536]{1,0:T(8,128)(2,1)S(1)}, bf16[64,1536]{1,0:T(8,128)(2,1)S(1)}, u32[]{:S(2)}, u32[]{:S(2)}) collective-permute-start(bf16[64,1536]{1,0:T(8,128)(2,1)S(1)} %get-tuple-element.12), channel_id=1, source_target_pairs={{0,1},{1,0},{2,3},{3,2},{4,5},{5,4},{6,7},{7,6},{8,9},{9,8},{10,11... | collective-permute-start | bytes 589832 | tf_op jit(solution)/shard_map/ppermute | solution.py:499
  4.9 9.4 %collective-permute-start.1 = (bf16[64,1536]{1,0:T(8,128)(2,1)S(1)}, bf16[64,1536]{1,0:T(8,128)(2,1)S(1)}, u32[]{:S(2)}, u32[]{:S(2)}) collective-permute-start(bf16[64,1536]{1,0:T(8,128)(2,1)S(1)} %get-tuple-element.13), channel_id=1, source_target_pairs={{1,2},{3,4},{5,6},{7,8},{9,10},{11,12},{13,14},{2,1},{4,3},{6,5},{... | collective-permute-start | bytes 589832 | tf_op jit(solution)/shard_map/ppermute | solution.py:497
  8.1 26.6 %all-to-all-start.1 = ((bf16[8,768,128]{2,1,0:T(8,128)(2,1)}), bf16[8,768,128]{2,1,0:T(8,128)(2,1)}, u32[]{:S(2)}, u32[]{:S(2)}) async-start(bf16[8,768,128]{2,1,0:T(8,128)(2,1)} %pack_kv.1), calls=%async_computation.1 | async-start | bytes 3145728 | tf_op jit(solution)/shard_map/all_to_all | solution.py:483
  14.4 0.9 copy-start.3
  34.7 9.1 %collective-permute-start.2 = (bf16[8,768,128]{2,1,0:T(8,128)(2,1)}, bf16[8,768,128]{2,1,0:T(8,128)(2,1)}, u32[]{:S(2)}, u32[]{:S(2)}) collective-permute-start(bf16[8,768,128]{2,1,0:T(8,128)(2,1)} %all-to-all-done.1.tie_ref.same_ref), channel_id=1, source_target_pairs={{0,1},{1,0},{2,3},{3,2},{4,5},{5,4},{6,7},{7,6},{8,9},{9,8},{10,11... | collective-permute-start | bytes 4718600 | tf_op jit(solution)/shard_map/ppermute | solution.py:507
  35.5 17.5 %all-to-all-start = ((bf16[8,192,256]{2,1,0:T(8,128)(2,1)}), bf16[8,192,256]{2,1,0:T(8,128)(2,1)S(1)}, u32[]{:S(2)}, u32[]{:S(2)}) async-start(bf16[8,192,256]{2,1,0:T(8,128)(2,1)} %get-tuple-element.14.q_ref), calls=%async_computation | async-start | bytes 1572864 | tf_op jit(solution)/shard_map/all_to_all | solution.py:483
  39.0 1.4 %copy-start.4 = (bf16[256,3072]{1,0:T(8,128)(2,1)S(1)}, bf16[256,3072]{1,0:T(8,128)(2,1)}, u32[]{:S(2)}) copy-start(bf16[256,3072]{1,0:T(8,128)(2,1)} %get-tuple-element.11.kv_ref) | copy-start | bytes 4718596
  104.1 19.4 %slice-start = ((s8[4718592]{0:T(1024)(128)(4,1)}), s8[4194304]{0:T(1024)(128)(4,1)S(1)}, s32[]{:S(2)}) async-start(s8[4718592]{0:T(1024)(128)(4,1)} %bitcast.2), calls=%async_computation.3 | async-start | bytes 8388608
  122.5 1.1 slice-start.1
